TPU v7x, 256 devices: a whole 4x4x8 slice. The times are simulated.
256 devices in a mesh: rows: 16 (over z_lo, x, core), rep: 16 (over y, z_hi).
Axes of the slice: x: 4, y: 4, z: 8 (z_hi: 4, z_lo: 2; z = z_hi * 2 + z_lo), core: 2. Of those that a mesh axis runs over, the one named last changes fastest.
Arguments:
- node_features: bfloat16 [32768, 256], P(('rows', 'rep')), may hold values from -6 to 6
- adjacency: bfloat16 [256, 64, 128, 128], P('rows', 'rep'), may hold values from -0.078125 to 0.078125
- column_ids: int32 [256, 64], P('rows', 'rep'), may hold values from 0 to 15
- block_counts: int32 [256, 16], P('rows', 'rep'), may hold values from 1 to 4, 40 in all within a row
- weight_first: bfloat16 [256, 512], replicated, may hold values from -0.375 to 0.375
- weight_second: bfloat16 [512, 256], replicated, may hold values from -0.25 to 0.25
- cotangent: bfloat16 [32768, 256], P(('rows', 'rep')), may hold values from -6 to 6
Outputs:
- embedding: bfloat16 [32768, 256], P(('rows', 'rep'))
- grad_first: float32 [256, 512], replicated
- grad_second: float32 [512, 256], replicated
Inputs may be any that keep to these rules, and one draw needn't show every extreme that they name: `block_counts`: each row block has 40 live slots over its 16 groups; some group of some row block has all 4 live.
All inputs are finite; a program needn't handle non-finite values.
Results may differ from a plain program's by a relative error of at most 0.024.
Values may be sent and summed in bfloat16 or wider, within the bound.
A program may use at most 64 MiB of HBM per device.

v0:
```python
import math
import jax
import jax.numpy as jnp
from jax import lax
from jax.sharding import PartitionSpec as P

BS = 128


def slot_weights(adjacency, block_counts, slot):
    weights = adjacency[:, slot]
    live_rows = slot < block_counts[:, 0]
    return jnp.where(live_rows[:, None, None], weights, jnp.zeros_like(weights))


def aggregate(node_field, adjacency, column_ids, block_counts):
    feature_width = node_field.shape[1]
    gathered = lax.all_gather(node_field, "rows", axis=0, tiled=True)
    blocks_in = gathered.reshape(-1, BS, feature_width)
    row_blocks = column_ids.shape[0]
    partial_sum = jnp.zeros((row_blocks, BS, feature_width), jnp.float32)
    for slot in range(column_ids.shape[1]):
        weights = slot_weights(adjacency, block_counts, slot)
        picked = blocks_in[column_ids[:, slot]]
        partial_sum = partial_sum + jnp.einsum(
            "rij,rjf->rif", weights, picked, preferred_element_type=jnp.float32
        )
    return lax.psum_scatter(
        partial_sum.reshape(row_blocks * BS, feature_width).astype(jnp.bfloat16),
        "rep",
        scatter_dimension=0,
        tiled=True,
    ).astype(jnp.float32)


def transpose_aggregate(cotangent, adjacency, column_ids, block_counts):
    feature_width = cotangent.shape[1]
    row_blocks = column_ids.shape[0]
    gathered = lax.all_gather(cotangent, "rep", axis=0, tiled=True).reshape(
        row_blocks, BS, feature_width
    )
    col_blocks = lax.axis_size("rows") * (cotangent.shape[0] // BS)
    summed = jnp.zeros((col_blocks, BS, feature_width), jnp.float32)
    for slot in range(column_ids.shape[1]):
        weights = slot_weights(adjacency, block_counts, slot)
        terms = jnp.einsum("rij,rif->rjf", weights, gathered, preferred_element_type=jnp.float32)
        summed = summed.at[column_ids[:, slot]].add(terms)
    return lax.psum_scatter(
        summed.reshape(col_blocks * BS, feature_width).astype(jnp.bfloat16),
        "rows",
        scatter_dimension=0,
        tiled=True,
    ).astype(jnp.float32)


def shards(
    node_features, adjacency, column_ids, block_counts, weight_first, weight_second, cotangent
):
    contract = (((0,), (0,)), ((), ()))
    mixed_input = aggregate(node_features, adjacency, column_ids, block_counts).astype(jnp.bfloat16)
    pre_first = jnp.dot(mixed_input, weight_first, preferred_element_type=jnp.float32)
    hidden = jax.nn.silu(pre_first).astype(jnp.bfloat16)
    second_in = jnp.dot(hidden, weight_second, preferred_element_type=jnp.float32).astype(
        jnp.bfloat16
    )
    embedding = aggregate(second_in, adjacency, column_ids, block_counts).astype(jnp.bfloat16)
    upstream = transpose_aggregate(cotangent, adjacency, column_ids, block_counts).astype(
        jnp.bfloat16
    )
    node_total = node_features.shape[0] * lax.axis_size("rows") * lax.axis_size("rep")
    scale_factor = 1.0 / math.sqrt(node_total)
    local_second = lax.dot_general(hidden, upstream, contract, preferred_element_type=jnp.float32)
    back_hidden = lax.dot_general(
        upstream, weight_second, (((1,), (1,)), ((), ())), preferred_element_type=jnp.float32
    )
    sigmoid_gate = jax.nn.sigmoid(pre_first)
    back_pre = (back_hidden * sigmoid_gate * (1.0 + pre_first * (1.0 - sigmoid_gate))).astype(
        jnp.bfloat16
    )
    local_first = lax.dot_general(
        mixed_input, back_pre, contract, preferred_element_type=jnp.float32
    )
    grad_first, grad_second = lax.psum((local_first, local_second), ("rows", "rep"))
    return (embedding, grad_first * scale_factor, grad_second * scale_factor)


def solution(mesh):
    in_specs = (
        P(("rows", "rep"), None),
        P("rows", "rep", None, None),
        P("rows", "rep"),
        P("rows", "rep"),
        P(),
        P(),
        P(("rows", "rep"), None),
    )
    out_specs = (P(("rows", "rep"), None), P(), P())
    return jax.shard_map(shards, mesh=mesh, in_specs=in_specs, out_specs=out_specs, check_vma=False)
```

profile of v0, /device:TPU:2, one launch (start us, length us, event | category | flops | bytes accessed | tf_op | source)
XLA Modules:
  0.0 649.3 jit_solution(16340234801673374021)
XLA Ops:
  10.2 37.3 %all-gather.4.cloned.1.call-done = bf16[2048,256]{1,0:T(8,128)(2,1)} async-done(((bf16[128,256]{1,0:T(8,128)(2,1)}), bf16[2048,256]{1,0:T(8,128)(2,1)}) %all-gather.4.cloned.1.call-update) | async-done | bytes 1048592 | tf_op jit(solution)/shard_map/all_gather | solution.py:18
  47.6 2.9 gather_fusion.2
  60.6 43.4 %all-gather.8.cloned.1.call-done = bf16[2048,256]{1,0:T(8,128)(2,1)} async-done(((bf16[128,256]{1,0:T(8,128)(2,1)}), bf16[2048,256]{1,0:T(8,128)(2,1)}) %all-gather.8.cloned.1.call-update) | async-done | bytes 1048592 | tf_op jit(solution)/shard_map/all_gather | solution.py:39
  104.0 3.3 fusion.16
  107.5 3.5 scatter_fusion
  111.1 3.1 fusion.13
  114.2 3.5 scatter_fusion.1
  117.7 3.1 fusion.19
  120.8 3.5 scatter_fusion.2
  124.4 3.1 fusion.22
  127.5 3.5 scatter_fusion.3
  132.2 58.8 %reduce-scatter.4.cloned.1.call-done = bf16[128,256]{1,0:T(8,128)(2,1)} async-done(((bf16[2048,256]{1,0:T(8,128)(2,1)}), bf16[128,256]{1,0:T(8,128)(2,1)}) %reduce-scatter.4.cloned.1.call-update) | async-done | bytes 65552 | tf_op jit(solution)/shard_map/reduce_scatter | solution.py:28
  193.1 58.3 %reduce-scatter.8.cloned.1.call-done = bf16[128,256]{1,0:T(8,128)(2,1)} async-done(((bf16[2048,256]{1,0:T(8,128)(2,1)}), bf16[128,256]{1,0:T(8,128)(2,1)}) %reduce-scatter.8.cloned.1.call-update) | async-done | bytes 65552 | tf_op jit(solution)/shard_map/reduce_scatter | solution.py:48
  251.4 1.9 fusion.12
  253.3 2.1 fusion.2
  255.5 34.7 %all-gather.6.cloned.1.call-done = bf16[2048,256]{1,0:T(8,128)(2,1)} async-done(((bf16[128,256]{1,0:T(8,128)(2,1)}), bf16[2048,256]{1,0:T(8,128)(2,1)}) %all-gather.6.cloned.1.call-update) | async-done | bytes 1048592 | tf_op jit(solution)/shard_map/all_gather | solution.py:18
  290.2 2.9 gather_fusion.6
  296.3 3.1 fusion.20
  301.3 1.8 fusion.14
  304.8 4.8 add_convert_fusion
  309.5 243.3 %all-reduce.3.cloned.1.call-done = (f32[256,512]{1,0:T(8,128)}, f32[512,256]{1,0:T(8,128)}) async-done(((f32[256,512]{1,0:T(8,128)}, f32[512,256]{1,0:T(8,128)}), (f32[256,512]{1,0:T(8,128)}, f32[512,256]{1,0:T(8,128)})) %all-reduce.3.cloned.1.call-update) | async-done | bytes 1048592 | tf_op jit(solution)/shard_map/psum | solution.py:83
  552.9 1.9 broadcast_multiply_fusion.1
  554.7 1.9 broadcast_multiply_fusion
  556.6 85.8 %reduce-scatter.6.cloned.1.call-done = bf16[128,256]{1,0:T(8,128)(2,1)} async-done(((bf16[2048,256]{1,0:T(8,128)(2,1)}), bf16[128,256]{1,0:T(8,128)(2,1)}) %reduce-scatter.6.cloned.1.call-update) | async-done | bytes 65552 | tf_op jit(solution)/shard_map/reduce_scatter | solution.py:28
  (59 shorter events, 23.2 us)
Async XLA Ops:
  7.2 185.0 %copy-start = (bf16[512,256]{1,0:T(8,128)(2,1)S(1)}, bf16[512,256]{1,0:T(8,128)(2,1)}, u32[]{:S(2)}) copy-start(bf16[512,256]{1,0:T(8,128)(2,1)} %param.12) | copy-start | bytes 786436
  7.2 40.4 %all-gather.4.cloned.1.call-start = ((), (), s32[]{:S(2)}) async-start(), calls=%async_computation.3 | async-start | bytes 1114112 | tf_op jit(solution)/shard_map/all_gather | solution.py:18
  7.9 96.1 %all-gather.8.cloned.1.call-start = ((), (), s32[]{:S(2)}) async-start(), calls=%async_computation.7 | async-start | bytes 1114112 | tf_op jit(solution)/shard_map/all_gather | solution.py:39
  8.7 182.4 %reduce-scatter.4.cloned.1.call-start = ((), (), s32[]{:S(2)}) async-start(), calls=%async_computation.4 | async-start | bytes 1114112 | tf_op jit(solution)/shard_map/reduce_scatter | solution.py:28
  47.6 2.9 copy-start.4
  52.1 3.2 copy-start.1
  55.3 1.8 copy-start.8
  57.1 1.2 copy-start.9
  57.6 1.3 copy-start.6
  60.5 190.9 %reduce-scatter.8.cloned.1.call-start = ((), (), s32[]{:S(2)}) async-start(), calls=%async_computation.8 | async-start | bytes 1114112 | tf_op jit(solution)/shard_map/reduce_scatter | solution.py:48
  107.5 3.5 copy-start.5
  131.0 60.1 %copy-start.11 = (bf16[256,512]{1,0:T(8,128)(2,1)S(1)}, bf16[256,512]{1,0:T(8,128)(2,1)}, u32[]{:S(2)}) copy-start(bf16[256,512]{1,0:T(8,128)(2,1)} %param.11) | copy-start | bytes 786436
  132.2 158.0 %all-gather.6.cloned.1.call-start = ((), (), s32[]{:S(2)}) async-start(), calls=%async_computation.5 | async-start | bytes 1114112 | tf_op jit(solution)/shard_map/all_gather | solution.py:18
  191.1 62.3 %copy-start.12 = (bf16[128,256]{1,0:T(8,128)(2,1)S(1)}, bf16[128,256]{1,0:T(8,128)(2,1)}, u32[]{:S(2)}) copy-start(bf16[128,256]{1,0:T(8,128)(2,1)} %reduce-scatter.4.cloned.1.call-done) | copy-start | bytes 196612
  193.0 359.8 %all-reduce.3.cloned.1.call-start = ((), (), s32[]{:S(2)}) async-start(), calls=%async_computation.9 | async-start | bytes 2097152 | tf_op jit(solution)/shard_map/psum | solution.py:83
  255.4 387.0 %reduce-scatter.6.cloned.1.call-start = ((), (), s32[]{:S(2)}) async-start(), calls=%async_computation.6 | async-start | bytes 1114112 | tf_op jit(solution)/shard_map/reduce_scatter | solution.py:28
  290.2 2.9 copy-start.3
  293.1 3.2 copy-start.2
  296.3 3.1 copy-start.10
  299.4 1.8 copy-start.7
Sparse Core Ops, SparseCore 0:
  9.9 37.6 all-gather.3
  50.0 53.9 all-gather.7
  107.5 83.4 reduce-scatter.3
  193.6 57.7 reduce-scatter.7
  253.7 36.4 all-gather.5
  296.2 256.5 all-reduce.2
  557.3 85.0 reduce-scatter.5
where the time goes:
time: 650 us; the launch traced here: 649 us
  waiting for transfers between devices  563 us (87%)
  matrix products  34.5 us (5%)
  other arithmetic  20.4 us (3%)
  local copies, waits for them, and re-layouts  16.5 us (3%)
  between operations  14.3 us (2%)
    psum x1, waiting for transfers between devices, shards(): lax.psum((local_first, local_second), ('rows', 'rep'))  243 us
    reduce_scatter x2, waiting for transfers between devices, aggregate(): lax.psum_scatter(partial_sum.reshape(row_blocks * BS, feature_width).asty...  145 us
    all_gather x2, waiting for transfers between devices, aggregate(): gathered = lax.all_gather(node_field, 'rows', axis=0, tiled=True)  72.1 us
    reduce_scatter x1, waiting for transfers between devices, transpose_aggregate(): lax.psum_scatter(summed.reshape(col_blocks * BS, feature_width).astype(jn...  58.3 us
    all_gather x1, waiting for transfers between devices, transpose_aggregate(): lax.all_gather(cotangent, 'rep', axis=0, tiled=True)  43.4 us
    dot_general x8, matrix products, aggregate(): jnp.einsum('rij,rjf->rif', weights, picked, preferred_element_type=jnp.fl...  15.9 us
    gather x8, local copies, waits for them, and re-layouts, aggregate(): picked = blocks_in[column_ids[:, slot]]  15.5 us
    scatter-add x4, other arithmetic, transpose_aggregate(): summed = summed.at[column_ids[:, slot]].add(terms)  14.1 us
  transfers between devices with their start and end apart: 7, of which 7 were waited for; matrix products, arithmetic and copies ran while one was open for 11% of the time, Pallas kernels for 0%

commit v1 on v0

--- a/solution.py
+++ b/solution.py
@@ -80,7 +80,7 @@
     local_first = lax.dot_general(
         mixed_input, back_pre, contract, preferred_element_type=jnp.float32
     )
-    grad_first, grad_second = lax.psum((local_first, local_second), ("rows", "rep"))
+    grad_first, grad_second = lax.psum(lax.psum((local_first, local_second), "rows"), "rep")
     return (embedding, grad_first * scale_factor, grad_second * scale_factor)
 
 

time: 650 us -> 689 us (1.060)
  waiting for transfers between devices: 563 us -> 608 us
  matrix products: 34.5 us -> 27.2 us
    psum x1 -> x2, waiting for transfers between devices: 243 us -> 282 us  [the longest x1 160 us: shards(): lax.psum(lax.psum((local_first, local_second), 'rows'), 'rep')]
    dot_general x8, matrix products: 15.9 us -> 8.63 us  [aggregate(): jnp.einsum('rij,rjf->rif', weights, picked, preferred_element_type=jnp.fl...]
  transfers between devices with their start and end apart: 7 -> 8, of which waited for: 7 -> 8; matrix products, arithmetic and copies ran while one was open for 11% -> 9% of each run, Pallas kernels for 0% -> 0%
where the time goes in v1:
time: 689 us; the launch traced here: 688 us
  waiting for transfers between devices  608 us (88%)
  matrix products  27.2 us (4%)
  other arithmetic  20.4 us (3%)
  local copies, waits for them, and re-layouts  17.9 us (3%)
  between operations  14.3 us (2%)
    psum x1, waiting for transfers between devices, shards(): lax.psum(lax.psum((local_first, local_second), 'rows'), 'rep')  160 us
    reduce_scatter x2, waiting for transfers between devices, aggregate(): lax.psum_scatter(partial_sum.reshape(row_blocks * BS, feature_width).asty...  143 us
    psum x1, waiting for transfers between devices, shards(): lax.psum((local_first, local_second), 'rows')  122 us
    all_gather x2, waiting for transfers between devices, aggregate(): gathered = lax.all_gather(node_field, 'rows', axis=0, tiled=True)  78.9 us
    reduce_scatter x1, waiting for transfers between devices, transpose_aggregate(): lax.psum_scatter(summed.reshape(col_blocks * BS, feature_width).astype(jn...  59.3 us
    all_gather x1, waiting for transfers between devices, transpose_aggregate(): lax.all_gather(cotangent, 'rep', axis=0, tiled=True)  43.5 us
    gather x8, local copies, waits for them, and re-layouts, aggregate(): picked = blocks_in[column_ids[:, slot]]  15.4 us
    scatter-add x4, other arithmetic, transpose_aggregate(): summed = summed.at[column_ids[:, slot]].add(terms)  14.1 us
  transfers between devices with their start and end apart: 8, of which 8 were waited for; matrix products, arithmetic and copies ran while one was open for 9% of the time, Pallas kernels for 0%

profile of v1, /device:TPU:2, one launch (start us, length us, event | category | flops | bytes accessed | tf_op | source)
XLA Modules:
  0.0 688.2 jit_solution(655920282865687233)
XLA Ops:
  10.2 37.3 %all-gather.4.cloned.1.call-done = bf16[2048,256]{1,0:T(8,128)(2,1)} async-done(((bf16[128,256]{1,0:T(8,128)(2,1)}), bf16[2048,256]{1,0:T(8,128)(2,1)}) %all-gather.4.cloned.1.call-update) | async-done | bytes 1048592 | tf_op jit(solution)/shard_map/all_gather | solution.py:18
  47.6 2.9 gather_fusion.2
  55.3 1.8 fusion.21
  60.5 43.5 %all-gather.8.cloned.1.call-done = bf16[2048,256]{1,0:T(8,128)(2,1)} async-done(((bf16[128,256]{1,0:T(8,128)(2,1)}), bf16[2048,256]{1,0:T(8,128)(2,1)}) %all-gather.8.cloned.1.call-update) | async-done | bytes 1048592 | tf_op jit(solution)/shard_map/all_gather | solution.py:39
  104.0 3.3 fusion.16
  107.5 3.5 scatter_fusion
  111.1 3.1 fusion.13
  114.2 3.5 scatter_fusion.1
  117.7 3.1 fusion.19
  120.9 3.5 scatter_fusion.2
  124.4 3.1 fusion.22
  127.5 3.5 scatter_fusion.3
  132.2 58.9 %reduce-scatter.4.cloned.1.call-done = bf16[128,256]{1,0:T(8,128)(2,1)} async-done(((bf16[2048,256]{1,0:T(8,128)(2,1)}), bf16[128,256]{1,0:T(8,128)(2,1)}) %reduce-scatter.4.cloned.1.call-update) | async-done | bytes 65552 | tf_op jit(solution)/shard_map/reduce_scatter | solution.py:28
  192.1 59.3 %reduce-scatter.8.cloned.1.call-done = bf16[128,256]{1,0:T(8,128)(2,1)} async-done(((bf16[2048,256]{1,0:T(8,128)(2,1)}), bf16[128,256]{1,0:T(8,128)(2,1)}) %reduce-scatter.8.cloned.1.call-update) | async-done | bytes 65552 | tf_op jit(solution)/shard_map/reduce_scatter | solution.py:48
  251.5 1.9 fusion.12
  253.4 2.1 fusion.2
  256.5 122.0 %all-reduce.7.cloned.1.call-done = (f32[256,512]{1,0:T(8,128)}, f32[512,256]{1,0:T(8,128)}) async-done(((f32[256,512]{1,0:T(8,128)}, f32[512,256]{1,0:T(8,128)}), (f32[256,512]{1,0:T(8,128)}, f32[512,256]{1,0:T(8,128)})) %all-reduce.7.cloned.1.call-update) | async-done | bytes 1048592 | tf_op jit(solution)/shard_map/psum | solution.py:83
  378.6 41.5 %all-gather.6.cloned.1.call-done = bf16[2048,256]{1,0:T(8,128)(2,1)} async-done(((bf16[128,256]{1,0:T(8,128)(2,1)}), bf16[2048,256]{1,0:T(8,128)(2,1)}) %all-gather.6.cloned.1.call-update) | async-done | bytes 1048592 | tf_op jit(solution)/shard_map/all_gather | solution.py:18
  420.1 2.9 gather_fusion.6
  427.8 1.8 fusion.20
  433.6 160.1 %all-reduce.5.cloned.1.call-done = (f32[256,512]{1,0:T(8,128)}, f32[512,256]{1,0:T(8,128)}) async-done(((f32[256,512]{1,0:T(8,128)}, f32[512,256]{1,0:T(8,128)}), (f32[256,512]{1,0:T(8,128)}, f32[512,256]{1,0:T(8,128)})) %all-reduce.5.cloned.1.call-update) | async-done | bytes 1048592 | tf_op jit(solution)/shard_map/psum | solution.py:83
  593.8 1.9 broadcast_multiply_fusion.1
  595.6 1.9 broadcast_multiply_fusion
  597.5 83.9 %reduce-scatter.6.cloned.1.call-done = bf16[128,256]{1,0:T(8,128)(2,1)} async-done(((bf16[2048,256]{1,0:T(8,128)(2,1)}), bf16[128,256]{1,0:T(8,128)(2,1)}) %reduce-scatter.6.cloned.1.call-update) | async-done | bytes 65552 | tf_op jit(solution)/shard_map/reduce_scatter | solution.py:28
  (62 shorter events, 23.4 us)
Async XLA Ops:
  7.2 246.2 %copy-start = (bf16[512,256]{1,0:T(8,128)(2,1)S(1)}, bf16[512,256]{1,0:T(8,128)(2,1)}, u32[]{:S(2)}) copy-start(bf16[512,256]{1,0:T(8,128)(2,1)} %param.12) | copy-start | bytes 786436
  7.2 40.4 %all-gather.4.cloned.1.call-start = ((), (), s32[]{:S(2)}) async-start(), calls=%async_computation.3 | async-start | bytes 1114112 | tf_op jit(solution)/shard_map/all_gather | solution.py:18
  7.9 96.1 %all-gather.8.cloned.1.call-start = ((), (), s32[]{:S(2)}) async-start(), calls=%async_computation.7 | async-start | bytes 1114112 | tf_op jit(solution)/shard_map/all_gather | solution.py:39
  8.7 182.4 %reduce-scatter.4.cloned.1.call-start = ((), (), s32[]{:S(2)}) async-start(), calls=%async_computation.4 | async-start | bytes 1114112 | tf_op jit(solution)/shard_map/reduce_scatter | solution.py:28
  47.6 2.9 copy-start.3
  52.1 3.2 copy-start.1
  55.3 1.8 copy-start.10
  57.1 1.2 copy-start.11
  57.6 1.3 copy-start.7
  60.5 191.0 %reduce-scatter.8.cloned.1.call-start = ((), (), s32[]{:S(2)}) async-start(), calls=%async_computation.8 | async-start | bytes 1114112 | tf_op jit(solution)/shard_map/reduce_scatter | solution.py:48
  107.5 3.5 copy-start.5
  131.0 60.1 %copy-start.12 = (bf16[256,512]{1,0:T(8,128)(2,1)S(1)}, bf16[256,512]{1,0:T(8,128)(2,1)}, u32[]{:S(2)}) copy-start(bf16[256,512]{1,0:T(8,128)(2,1)} %param.11) | copy-start | bytes 786436
  132.2 246.3 %all-reduce.7.cloned.1.call-start = ((), (), s32[]{:S(2)}) async-start(), calls=%async_computation.10 | async-start | bytes 2097152 | tf_op jit(solution)/shard_map/psum | solution.py:83
  255.5 164.6 %all-gather.6.cloned.1.call-start = ((), (), s32[]{:S(2)}) async-start(), calls=%async_computation.5 | async-start | bytes 1114112 | tf_op jit(solution)/shard_map/all_gather | solution.py:18
  256.4 337.3 %all-reduce.5.cloned.1.call-start = ((), (), s32[]{:S(2)}) async-start(), calls=%async_computation.9 | async-start | bytes 2097152 | tf_op jit(solution)/shard_map/psum | solution.py:83
  378.5 302.9 %reduce-scatter.6.cloned.1.call-start = ((), (), s32[]{:S(2)}) async-start(), calls=%async_computation.6 | async-start | bytes 1114112 | tf_op jit(solution)/shard_map/reduce_scatter | solution.py:28
  420.1 2.9 copy-start.4
  424.6 3.2 copy-start.2
  427.8 1.8 copy-start.9
  429.6 1.2 copy-start.8
  430.8 1.2 copy-start.6
Sparse Core Ops, SparseCore 0:
  9.9 37.6 all-gather.3
  50.0 53.9 all-gather.7
  107.5 83.5 reduce-scatter.3
  193.6 57.7 reduce-scatter.7
  255.6 122.8 all-reduce.6
  380.9 39.1 all-gather.5
  422.9 170.7 all-reduce.4
  597.8 83.5 reduce-scatter.5
